TPU v7x, 32 devices: a whole 2x2x4 slice. The times are simulated.
32 devices in a mesh: groups: 2 (over y), ctx: 4 (over z), dp: 2 (over x), mp: 2 (over core).
Axes of the slice: x: 2, y: 2, z: 4, core: 2. Of those that a mesh axis runs over, the one named last changes fastest.
Arguments:
- head_inputs: bfloat16 [3, 4, 1024, 1536], P(None, ('groups', 'dp'), 'ctx', 'mp'), parts along dimension 1, may hold values from -0.29882812 to 0.29882812
- write_read: bfloat16 [3, 4, 1024, 128], P(None, ('groups', 'dp'), 'ctx'), parts along dimension 1, may hold values from -0.26953125 to 0.26953125
- decay_steps: int32 [3, 4, 12, 1024], P(None, ('groups', 'dp'), 'mp', 'ctx'), parts along dimension 1, may hold values from 0 to 512
- scan_orders: int32 [2, 4, 1024], P(None, ('groups', 'dp'), 'ctx'), parts along dimension 1, may hold values from 0 to 1023, as said below
- cotangent: bfloat16 [4, 1024, 768], P(('groups', 'dp'), 'ctx'), parts along dimension 0, may hold values from -0.59765625 to 0.59765625
- out_weight: bfloat16 [3, 768, 1536], P(None, 'ctx', 'mp'), may hold values from -0.4375 to 0.4375
Outputs:
- grad_inputs: bfloat16 [3, 4, 1024, 1536], P(None, ('groups', 'dp'), 'ctx', 'mp'), parts along dimension 1
- grad_write_read: bfloat16 [3, 4, 1024, 128], P(None, ('groups', 'dp'), 'ctx'), parts along dimension 1
- grad_weight: bfloat16 [6, 768, 1536], P('groups', 'ctx', 'mp'), parts along dimension 0
There are 2 independent parts, one for each index of `groups`. A program takes and returns all parts, laid end to end along the dimension named above; an argument that names none is the same for every part. Nothing has to cross between parts.
Inputs may be any that keep to these rules, and one draw needn't show every extreme that they name: `scan_orders`: for every volume and each of the two orders, position d * 256 + q * 64 + m (0 <= m < 64) holds a patch of index q * 256 + d * 64 + m' with 0 <= m' < 64; every patch stands at exactly one position.
All inputs are finite; a program needn't handle non-finite values.
Results may differ from a plain program's by a relative error of at most 0.005.
Values may be sent and summed in bfloat16 or wider, within the bound.
A program may use at most 128 MiB of HBM per device.

v0:
```python
import math
import jax
import jax.numpy as jnp
from jax import lax
from jax.sharding import PartitionSpec as P

P_SIZE = 128
N = 64
EXACT = lax.Precision.HIGHEST


def prefix(value, axis, join, neutral, backward):
    count, mine = (lax.axis_size(axis), lax.axis_index(axis))
    pieces = jax.tree.map(lambda part: lax.all_gather(part, axis), value)
    if backward:
        pieces = jax.tree.map(lambda part: part[::-1], pieces)
        mine = count - 1 - mine
    running = jax.tree.map(
        lambda part, zero: jnp.full_like(part, 0) + jnp.asarray(zero, part.dtype), value, neutral
    )

    def lap(position, running):
        longer = join(running, jax.tree.map(lambda part: part[position], pieces))
        return jax.tree.map(lambda new, old: jnp.where(position < mine, new, old), longer, running)

    return lax.fori_loop(0, count - 1, lap, running)


def contract(form, *operands):
    return jnp.einsum(form, *operands, precision=EXACT)


def segment_parts(log_rates, writes, readers):
    running = jnp.cumsum(log_rates, axis=-1)
    final_log = running[..., -1]
    length = log_rates.shape[-1]
    causal = jnp.arange(length)[:, None] >= jnp.arange(length)[None, :]
    differ = jnp.where(causal, running[..., :, None] - running[..., None, :], 0.0)
    decay_mat = jnp.where(causal, jnp.exp(differ), 0.0)
    scores = contract("ovin,ovjn->ovij", readers, writes)
    mixing = scores[:, :, None] * decay_mat
    return (running, final_log, decay_mat, mixing)


def segment_forward(pieces, signal, writes, readers, memory):
    running, final_log, decay_mat, mixing = pieces
    rising = jnp.exp(running)
    falling = jnp.exp(final_log[..., None] - running)
    outputs = contract("ovhij,ovjhp->ovihp", mixing, signal) + contract(
        "ovhi,ovin,ovhnp->ovihp", rising, readers, memory
    )
    memory_next = jnp.exp(final_log)[..., None, None] * memory + contract(
        "ovhj,ovjn,ovjhp->ovhnp", falling, writes, signal
    )
    return (outputs, memory_next)


def segment_backward(pieces, signal, writes, readers, upstream, memory, memory_grad):
    running, final_log, decay_mat, mixing = pieces
    rising = jnp.exp(running)
    falling = jnp.exp(final_log[..., None] - running)
    grad_signal = contract("ovhij,ovihp->ovjhp", mixing, upstream) + contract(
        "ovhj,ovjn,ovhnp->ovjhp", falling, writes, memory_grad
    )
    weighted = contract("ovihp,ovjhp->ovhij", upstream, signal) * decay_mat
    grad_writes = contract("ovhij,ovin->ovjn", weighted, readers) + contract(
        "ovhj,ovjhp,ovhnp->ovjn", falling, signal, memory_grad
    )
    grad_readers = contract("ovhij,ovjn->ovin", weighted, writes) + contract(
        "ovhi,ovihp,ovhnp->ovin", rising, upstream, memory
    )
    grad_prev = jnp.exp(final_log)[..., None, None] * memory_grad + contract(
        "ovhi,ovin,ovihp->ovhnp", rising, readers, upstream
    )
    return (grad_signal, grad_writes, grad_readers, grad_prev)


def run_segments(signal, writes, readers, log_rates, upstream, memory_in, grad_in, length):
    blocks = signal.shape[2] // length

    def cut_rows(array, number, along):
        start_row = (number * length).astype(jnp.int32)
        return lax.dynamic_slice_in_dim(array, start_row, length, along)

    def forward_turn(number, carried):
        memory, outputs, memories = carried
        sig = cut_rows(signal, number, 2)
        wri = cut_rows(writes, number, 2)
        rea = cut_rows(readers, number, 2)
        pieces = segment_parts(cut_rows(log_rates, number, 3), wri, rea)
        out_rows, memory_next = segment_forward(pieces, sig, wri, rea, memory)
        outputs = lax.dynamic_update_slice_in_dim(
            outputs, out_rows, (number * length).astype(jnp.int32), 2
        )
        memories = lax.dynamic_update_index_in_dim(memories, memory, number, 0)
        return (memory_next, outputs, memories)

    start_memories = jnp.zeros((blocks,) + memory_in.shape, memory_in.dtype)
    _, outputs, memories = lax.fori_loop(
        0, blocks, forward_turn, (memory_in, jnp.zeros_like(signal), start_memories)
    )

    def backward_turn(countdown, carried):
        memory_grad, grad_signal, grad_writes, grad_readers = carried
        number = blocks - 1 - countdown
        sig = cut_rows(signal, number, 2)
        wri = cut_rows(writes, number, 2)
        rea = cut_rows(readers, number, 2)
        pieces = segment_parts(cut_rows(log_rates, number, 3), wri, rea)
        memory = lax.dynamic_index_in_dim(memories, number, 0, keepdims=False)
        part_sig, part_wri, part_rea, grad_prev = segment_backward(
            pieces, sig, wri, rea, cut_rows(upstream, number, 2), memory, memory_grad
        )
        start_row = (number * length).astype(jnp.int32)
        grad_signal = lax.dynamic_update_slice_in_dim(grad_signal, part_sig, start_row, 2)
        grad_writes = lax.dynamic_update_slice_in_dim(grad_writes, part_wri, start_row, 2)
        grad_readers = lax.dynamic_update_slice_in_dim(grad_readers, part_rea, start_row, 2)
        return (grad_prev, grad_signal, grad_writes, grad_readers)

    _, grad_signal, grad_writes, grad_readers = lax.fori_loop(
        0,
        blocks,
        backward_turn,
        (grad_in, jnp.zeros_like(signal), jnp.zeros_like(writes), jnp.zeros_like(readers)),
    )
    return (outputs, grad_signal, grad_writes, grad_readers)


def carry_forward(earlier, later):
    return (earlier[0] + later[0], jnp.exp(later[0])[..., None, None] * earlier[1] + later[1])


def carry_backward(earlier, later):
    return (earlier[0] + later[0], later[1] + jnp.exp(later[0])[..., None, None] * earlier[1])


def shards(head_inputs, write_read, decay_steps, scan_orders, cotangent, out_weight):
    volumes, tokens, model_width = cotangent.shape
    ctx_count = lax.axis_size("ctx")
    seq_len = tokens * ctx_count
    local_heads = decay_steps.shape[2]
    inner_width = head_inputs.shape[3]
    gathered = lax.all_gather(cotangent, "ctx", axis=1, tiled=True)

    def reorder(ordering):
        return jax.vmap(lambda table_rows, row_ids: table_rows[row_ids])(gathered, ordering)

    scanned = jnp.stack([cotangent, reorder(scan_orders[0]), reorder(scan_orders[1])])
    upstream = jnp.einsum(
        "ovtd,odi->ovti",
        scanned,
        lax.all_gather(out_weight, "ctx", axis=1, tiled=True),
        preferred_element_type=jnp.float32,
    ).astype(jnp.bfloat16)
    upstream = lax.optimization_barrier(upstream)
    signal = head_inputs.astype(jnp.float32).reshape(3, volumes, tokens, local_heads, P_SIZE)
    grad_up = upstream.astype(jnp.float32).reshape(3, volumes, tokens, local_heads, P_SIZE)
    writes = write_read[..., :N].astype(jnp.float32)
    readers = write_read[..., N:].astype(jnp.float32)
    log_rates = -decay_steps.astype(jnp.float32) / seq_len
    running = jnp.cumsum(log_rates, axis=-1)
    summed_log = running[..., -1]
    end_state = contract(
        "ovht,ovtn,ovthp->ovhnp", jnp.exp(summed_log[..., None] - running), writes, signal
    )
    start_grad = contract("ovht,ovtn,ovthp->ovhnp", jnp.exp(running), readers, grad_up)
    zeros_log = jnp.zeros_like(summed_log)
    zeros_state = jnp.zeros_like(end_state)
    _, state_in = prefix(
        (summed_log, end_state), "ctx", carry_forward, (zeros_log, zeros_state), False
    )
    _, grad_out = prefix(
        (summed_log, start_grad), "ctx", carry_backward, (zeros_log, zeros_state), True
    )
    length = math.gcd(tokens, 128)
    outputs, grad_signal, grad_writes, grad_readers = run_segments(
        signal, writes, readers, log_rates, grad_up, state_in, grad_out, length
    )
    grad_wr = lax.psum(jnp.concatenate([grad_writes, grad_readers], axis=-1), "mp").astype(
        jnp.bfloat16
    )
    grad_inputs = grad_signal.reshape(3, volumes, tokens, inner_width).astype(jnp.bfloat16)
    outputs_bf = outputs.reshape(3, volumes, tokens, inner_width).astype(jnp.bfloat16)
    weight_term = jnp.einsum(
        "ovtd,ovti->odi", scanned, outputs_bf, preferred_element_type=jnp.float32
    )
    rows_sum = lax.psum_scatter(weight_term, "ctx", scatter_dimension=1, tiled=True)
    weight_grad = lax.psum(rows_sum, "dp").astype(jnp.bfloat16)
    return (grad_inputs, grad_wr, weight_grad)


def solution(mesh):
    in_specs = (
        P(None, ("groups", "dp"), "ctx", "mp"),
        P(None, ("groups", "dp"), "ctx", None),
        P(None, ("groups", "dp"), "mp", "ctx"),
        P(None, ("groups", "dp"), "ctx"),
        P(("groups", "dp"), "ctx", None),
        P(None, "ctx", "mp"),
    )
    out_specs = (
        P(None, ("groups", "dp"), "ctx", "mp"),
        P(None, ("groups", "dp"), "ctx", None),
        P("groups", "ctx", "mp"),
    )
    return jax.shard_map(shards, mesh=mesh, in_specs=in_specs, out_specs=out_specs, check_vma=False)
```

profile of v0, /device:TPU:0, one launch (start us, length us, event | category | flops | bytes accessed | tf_op | source)
XLA Modules:
  0.0 406.5 jit_solution(13065868097995965039)
XLA Ops:
  8.0 0.7 fusion.84
  8.7 5.4 %reduce-window.6 = f32[3,1,6,2,128]{4,3,2,1,0:T(2,128)S(1)} reduce-window(f32[3,1,6,2,128]{4,3,2,1,0:T(2,128)S(1)} %bitcast.295, f32[]{:T(128)} %constant.173.clone.1), window={size=1x1x1x1x128 pad=0_0x0_0x0_0x0_0x127_0}, to_apply=%region_0.0 | reduce-window | flops 585216 | bytes 36868 | tf_op jit(solution)/shard_map/reduce-window
  14.6 1.1 fusion.94
  17.6 0.8 convert_bitcast_fusion.1
  18.4 2.2 fusion.72
  21.5 1.7 copy.120
  23.2 14.1 %all-gather.1 = f32[12,1,6,1]{2,3,1,0:T(1,128)} all-gather(f32[3,1,6,1]{2,3,1,0:T(1,128)S(1)} %copy.107), channel_id=3, replica_groups=mesh['groups'=2,'ctx'=4,'dp'=2,'mp'=2] {'ctx'}, dimensions={0}, use_global_device_ids=true | all-gather | bytes 360 | tf_op jit(solution)/shard_map/all_gather | solution.py:14
  37.3 12.2 %all-gather.8.cloned.1.call-done = bf16[1,1024,768]{2,1,0:T(8,128)(2,1)} async-done(((bf16[1,256,768]{2,1,0:T(8,128)(2,1)}), bf16[1,1024,768]{2,1,0:T(8,128)(2,1)}) %all-gather.8.cloned.1.call-update) | async-done | bytes 1572880 | tf_op jit(solution)/shard_map/all_gather | solution.py:143
  49.6 3.6 gather_fusion
  53.2 2.9 gather_fusion.1
  56.1 45.0 %all-gather.14.cloned.1.call-done = f32[12,6,64,128]{3,2,1,0:T(8,128)} async-done(((f32[3,6,64,128]{3,2,1,0:T(8,128)}), f32[12,6,64,128]{3,2,1,0:T(8,128)}) %all-gather.14.cloned.1.call-update) | async-done | bytes 2359312 | tf_op jit(solution)/shard_map/all_gather | solution.py:14
  101.1 5.7 %while.69 = (s32[]{:T(128)}, f32[3,1,6,64,128]{4,3,2,1,0:T(8,128)S(1)}, s32[]{:T(128)}, f32[4,3,1,6]{3,2,1,0:T(1,128)}, f32[4,3,1,6,64,128]{5,4,3,1,2,0:T(8,128)}, /*index=5*/s32[]{:T(128)}, s32[]{:T(128)}) while((s32[]{:T(128)}, f32[3,1,6,64,128]{4,3,2,1,0:T(8,128)S(1)}, s32[]{:T(128)}, f32[4,3,1,6]{3,2,1,0:T(1,128)}, ...), condition=%wide.region_5.6_spmd.clone, body=%wide.region_4.5_spmd.clone.sunk | while | flops 589828 | bytes 1769937 | solution.py:26
  101.8 1.2 fusion.187
  103.7 1.2 fusion.187
  105.6 1.2 fusion.187
  106.8 64.7 %all-gather.10.cloned.1.call-done = bf16[3,768,768]{2,1,0:T(8,128)(2,1)} async-done(((bf16[3,192,768]{2,1,0:T(8,128)(2,1)}), bf16[3,768,768]{2,1,0:T(8,128)(2,1)}) %all-gather.10.cloned.1.call-update) | async-done | bytes 3538960 | tf_op jit(solution)/shard_map/all_gather | solution.py:152
  171.5 3.3 fusion.71
  174.8 1.5 copy.104
  176.3 3.5 fusion.74
  180.2 27.0 %while.66 = (s32[]{:T(128)}, f32[3,1,6,64,128]{4,3,2,0,1:T(8,128)S(1)}, bf16[3,1,256,6,128]{2,4,3,0,1:T(8,128)(2,1)S(1)}, f32[2,3,1,6,64,128]{5,4,3,1,2,0:T(8,12...) while((s32[]{:T(128)}, ...), condition=%wide.region_8.9_spmd, body=%wide.region_6.8_spmd.sunk | while | flops 946094080 | bytes 10168943 | solution.py:99
  180.2 1.3 constant_dynamic-slice_fusion.10
  181.5 1.9 reduce_window_sum.68
  183.7 0.9 dynamic-slice_bitcast_fusion.6
  184.6 2.0 convolution_bitcast_fusion.8
  187.1 3.9 fusion.159
  191.2 2.5 fusion.157
  193.7 1.3 constant_dynamic-slice_fusion.10
  195.0 1.9 reduce_window_sum.68
  197.2 0.9 dynamic-slice_bitcast_fusion.6
  198.1 2.0 convolution_bitcast_fusion.8
  200.6 3.9 fusion.159
  204.6 2.5 fusion.157
  207.2 5.7 %fusion.82 = f32[3,768,768]{2,1,0:T(8,128)} fusion(bf16[3,256,768]{1,2,0:T(8,128)(2,1)S(1)} %bitcast.282, bf16[1,1,256,768]{3,2,0,1:T(8,128)(2,1)} %bitcast.290, bf16[1,1,256,768]{3,2,0,1:T(8,128)(2,1)S(1)} %bitcast.288, bf16[1,1,256,768]{3,2,0,1:T(8,128)(2,1)} %bitcast.292), kind=kOutput, calls=%fused_computation.120 | convolution fusion | flops 907149312 | bytes 9437184 | tf_op jit(solution)/shard_map/ovtd,ovti->odi/dot_general | solution.py:184
  214.2 1.8 copy.109
  216.0 13.1 %all-gather.12.cloned.1.call-done = f32[12,6,64,128]{3,2,1,0:T(8,128)} async-done(((f32[3,6,64,128]{3,2,1,0:T(8,128)}), f32[12,6,64,128]{3,2,1,0:T(8,128)}) %all-gather.12.cloned.1.call-update) | async-done | bytes 2359312 | tf_op jit(solution)/shard_map/all_gather | solution.py:14
  229.1 1.8 rev.6
  231.7 0.7 broadcast.217
  233.1 41.1 %while.67 = (s32[]{:T(128)}, f32[3,1,6,64,128]{4,3,2,0,1:T(8,128)S(1)}, bf16[3,1,256,6,128]{2,4,3,0,1:T(8,128)(2,1)S(1)}, f32[3,1,256,64]{2,3,0,1:T(8,128)}, f32...) while((s32[]{:T(128)}, ...), condition=%wide.region_12.13_spmd, body=%wide.region_9.12_spmd.sunk | while | flops 1929625600 | bytes 41488220 | solution.py:120
  233.1 0.9 reduce_window_sum.69
  234.1 1.1 dynamic-slice_bitcast_fusion.7
  235.2 2.0 convolution_bitcast_fusion.9
  237.9 1.7 fusion.178
  239.6 1.0 copy-done.5
  241.0 2.3 fusion.182
  243.3 3.7 fusion.180
  247.5 2.6 fusion.179
  250.2 2.4 fusion.176
  252.6 0.9 fusion.181
  253.6 0.8 reduce_window_sum.69
  254.6 1.1 dynamic-slice_bitcast_fusion.7
  255.7 2.0 convolution_bitcast_fusion.9
  258.4 1.7 fusion.178
  260.1 1.0 copy-done.5
  261.5 2.3 fusion.182
  263.8 3.7 fusion.180
  268.0 2.7 fusion.179
  270.7 2.4 fusion.176
  273.2 0.9 fusion.181
  274.1 1.1 copy.121
  275.2 1.1 copy.122
  276.5 1.5 copy.125
  278.0 5.0 %all-reduce.2 = bf16[3,1,256,128]{3,2,1,0:T(8,128)(2,1)} all-reduce(f32[3,1,256,128]{3,2,1,0:T(8,128)S(1)} %pad_maximum_fusion), channel_id=1, replica_groups=mesh['groups'=2,'ctx'=4,'dp'=2,'mp'=2] {'mp'}, use_global_device_ids=true, to_apply=%region_13.14 | all-reduce | flops 98304 | bytes 589824 | tf_op jit(solution)/shard_map/psum | solution.py:179
  283.0 70.6 %reduce-scatter.2.cloned.1.call-done = f32[3,192,768]{2,1,0:T(8,128)} async-done(((f32[3,768,768]{2,1,0:T(8,128)}), f32[3,192,768]{2,1,0:T(8,128)}) %reduce-scatter.2.cloned.1.call-update) | async-done | bytes 1769488 | tf_op jit(solution)/shard_map/reduce_scatter | solution.py:187
  353.6 46.3 %all-reduce.3 = bf16[3,192,768]{2,1,0:T(8,128)(2,1)} all-reduce(f32[3,192,768]{2,1,0:T(8,128)} %reduce-scatter.2.cloned.1.call-done), channel_id=1, replica_groups=mesh['groups'=2,'ctx'=4,'dp'=2,'mp'=2] {'dp'}, use_global_device_ids=true, to_apply=%region_15.16 | all-reduce | flops 442368 | bytes 2654208 | tf_op jit(solution)/shard_map/psum | solution.py:188
  (121 shorter events, 14.7 us)
Async XLA Ops:
  7.2 8.9 %copy-start.10 = (bf16[3,1,256,768]{3,2,1,0:T(8,128)(2,1)S(1)}, bf16[3,1,256,768]{3,2,1,0:T(8,128)(2,1)}, u32[]{:S(2)}) copy-start(bf16[3,1,256,768]{3,2,1,0:T(8,128)(2,1)} %param.14) | copy-start | bytes 3538948
  7.2 42.4 %all-gather.8.cloned.1.call-start = ((), (), s32[]{:S(2)}) async-start(), calls=%async_computation.1 | async-start | bytes 1966080 | tf_op jit(solution)/shard_map/all_gather | solution.py:143
  7.9 93.2 %all-gather.14.cloned.1.call-start = ((), (), s32[]{:S(2)}) async-start(), calls=%async_computation.5 | async-start | bytes 2949120 | tf_op jit(solution)/shard_map/all_gather | solution.py:14
  8.7 8.0 %copy-start.8 = (f32[3,1,6,256]{3,2,1,0:T(8,128)}, f32[3,1,6,256]{3,2,1,0:T(8,128)S(1)}, u32[]{:S(2)}) copy-start(f32[3,1,6,256]{3,2,1,0:T(8,128)S(1)} %fusion.84) | copy-start | bytes 55300
  20.6 150.9 %all-gather.10.cloned.1.call-start = ((), (), s32[]{:S(2)}) async-start(), calls=%async_computation.2 | async-start | bytes 4423680 | tf_op jit(solution)/shard_map/all_gather | solution.py:152
  21.3 207.8 %all-gather.12.cloned.1.call-start = ((), (), s32[]{:S(2)}) async-start(), calls=%async_computation.4 | async-start | bytes 2949120 | tf_op jit(solution)/shard_map/all_gather | solution.py:14
  21.5 15.8 %copy-start.14 = (s32[2,1,256]{2,1,0:T(1,128)S(1)}, s32[2,1,256]{2,1,0:T(1,128)}, u32[]{:S(2)}) copy-start(s32[2,1,256]{2,1,0:T(1,128)} %param.17) | copy-start | bytes 6148
  49.6 3.7 copy-start.1
  101.1 70.4 %copy-start.7 = (bf16[256,768]{1,0:T(8,128)(2,1)S(1)}, bf16[256,768]{1,0:T(8,128)(2,1)}, u32[]{:S(2)}) copy-start(bf16[256,768]{1,0:T(8,128)(2,1)} %gather_fusion) | copy-start | bytes 1179652
  174.8 1.5 copy-start.3
  179.8 173.8 %reduce-scatter.2.cloned.1.call-start = ((), (), s32[]{:S(2)}) async-start(), calls=%async_computation.3 | async-start | bytes 8847360 | tf_op jit(solution)/shard_map/reduce_scatter | solution.py:187
  207.2 5.8 %copy-start.2 = (f32[2,3,1,6,64,128]{5,4,3,1,2,0:T(8,128)}, f32[2,3,1,6,64,128]{5,4,3,1,2,0:T(8,128)S(1)}, u32[]{:S(2)}) copy-start(f32[2,3,1,6,64,128]{5,4,3,1,2,0:T(8,128)S(1)} %get-tuple-element.1132) | copy-start | bytes 3538948
  212.9 0.7 copy-start.13
  212.9 1.3 copy-start.4
  231.5 1.5 copy-start.9
  234.1 3.6 copy-start
  239.6 1.0 copy-start.5
  243.3 3.7 copy-start.11
  247.5 2.6 copy-start.12
  250.2 3.4 copy-start.6
  254.6 3.6 copy-start
  260.1 1.0 copy-start.5
  263.8 3.7 copy-start.11
  268.0 2.7 copy-start.12
  270.7 3.4 copy-start.6
Sparse Core Ops, SparseCore 0:
  9.6 39.9 all-gather.7
  51.7 49.3 all-gather.13
  102.7 68.7 all-gather.9
  180.0 49.1 all-gather.11
  231.3 122.3 reduce-scatter.1
where the time goes:
time: 408 us; the launch traced here: 406 us
  waiting for transfers between devices  207 us (51%)
  matrix products  66.1 us (16%)
  blocking collectives  65.4 us (16%)
  local copies, waits for them, and re-layouts  35.1 us (9%)
  other arithmetic  18 us (4%)
  between operations  14 us (3%)
    reduce_scatter x1, waiting for transfers between devices, shards(): lax.psum_scatter(weight_term, 'ctx', scatter_dimension=1, tiled=True)  70.6 us
    all_gather x1, waiting for transfers between devices, shards(): lax.all_gather(out_weight, 'ctx', axis=1, tiled=True)  64.7 us
    all_gather x2, waiting for transfers between devices, prefix(): pieces = jax.tree.map(lambda part: lax.all_gather(part, axis), value)  58.1 us
    dot_general x28, matrix products, contract(): return jnp.einsum(form, *operands, precision=EXACT)  57 us
    psum x1, blocking collectives, shards(): weight_grad = lax.psum(rows_sum, 'dp').astype(jnp.bfloat16)  46.3 us
    all_gather x1, blocking collectives, prefix(): pieces = jax.tree.map(lambda part: lax.all_gather(part, axis), value)  14.1 us
    all_gather x1, waiting for transfers between devices, shards(): gathered = lax.all_gather(cotangent, 'ctx', axis=1, tiled=True)  12.2 us
  transfers between devices with their start and end apart: 5, of which 5 were waited for; matrix products, arithmetic and copies ran while one was open for 26% of the time, Pallas kernels for 0%

commit v1 on v0

--- a/solution.py
+++ b/solution.py
@@ -140,7 +140,12 @@
     seq_len = tokens * ctx_count
     local_heads = decay_steps.shape[2]
     inner_width = head_inputs.shape[3]
-    gathered = lax.all_gather(cotangent, "ctx", axis=1, tiled=True)
+    ring = [cotangent]
+    for hop in range(3):
+        ring.append(lax.ppermute(ring[-1], "ctx", [(dev, (dev + 1) % 4) for dev in range(4)]))
+    gathered = jnp.roll(
+        jnp.concatenate(ring[::-1], axis=1), (lax.axis_index("ctx") + 1) * ring[0].shape[1], axis=1
+    )
 
     def reorder(ordering):
         return jax.vmap(lambda table_rows, row_ids: table_rows[row_ids])(gathered, ordering)

time: 408 us -> 395 us (0.968)
  waiting for transfers between devices: 207 us -> 163 us
  blocking collectives: 65.4 us -> 86.8 us
  starting transfers between devices: 0.38 us -> 5.53 us
    all_gather x2, waiting for transfers between devices: 58.1 us -> 13.1 us  [prefix(): pieces = jax.tree.map(lambda part: lax.all_gather(part, axis), value)]
    ppermute x0 -> x3, waiting for transfers between devices: none -> 26.6 us  [shards(): lax.ppermute(ring[-1], 'ctx', [(dev, (dev + 1) % 4) for dev in range(4)])]
    all_gather x1, blocking collectives: 14.1 us -> 35.5 us  [prefix(): pieces = jax.tree.map(lambda part: lax.all_gather(part, axis), value)]
    all_gather x1, waiting for transfers between devices: 64.7 us -> 52.4 us  [shards(): lax.all_gather(out_weight, 'ctx', axis=1, tiled=True)]
    all_gather x1 -> x0, waiting for transfers between devices: 12.2 us -> none  [shards(): gathered = lax.all_gather(cotangent, 'ctx', axis=1, tiled=True)]
    ppermute x0 -> x3, starting transfers between devices: none -> 5.19 us  [shards(): lax.ppermute(ring[-1], 'ctx', [(dev, (dev + 1) % 4) for dev in range(4)])]
    unnamed x24 -> x31, local copies, waits for them, and re-layouts: 3.73 us -> 8.07 us
  transfers between devices with their start and end apart: 5 -> 7, of which waited for: 5 -> 5; matrix products, arithmetic and copies ran while one was open for 26% -> 25% of each run, Pallas kernels for 0% -> 0%
where the time goes in v1:
time: 395 us; the launch traced here: 393 us
  waiting for transfers between devices  163 us (41%)
  blocking collectives  86.8 us (22%)
  matrix products  66.1 us (17%)
  local copies, waits for them, and re-layouts  38.8 us (10%)
  other arithmetic  18.1 us (5%)
  between operations  14 us (4%)
  starting transfers between devices  5.53 us (1%)
    reduce_scatter x1, waiting for transfers between devices, shards(): lax.psum_scatter(weight_term, 'ctx', scatter_dimension=1, tiled=True)  70.6 us
    dot_general x28, matrix products, contract(): return jnp.einsum(form, *operands, precision=EXACT)  57 us
    all_gather x1, waiting for transfers between devices, shards(): lax.all_gather(out_weight, 'ctx', axis=1, tiled=True)  52.4 us
    psum x1, blocking collectives, shards(): weight_grad = lax.psum(rows_sum, 'dp').astype(jnp.bfloat16)  46.3 us
    all_gather x1, blocking collectives, prefix(): pieces = jax.tree.map(lambda part: lax.all_gather(part, axis), value)  35.5 us
    ppermute x3, waiting for transfers between devices, shards(): lax.ppermute(ring[-1], 'ctx', [(dev, (dev + 1) % 4) for dev in range(4)])  26.6 us
    all_gather x2, waiting for transfers between devices, prefix(): pieces = jax.tree.map(lambda part: lax.all_gather(part, axis), value)  13.1 us
    unnamed x31, local copies, waits for them, and re-layouts  8.07 us
  transfers between devices with their start and end apart: 7, of which 5 were waited for; matrix products, arithmetic and copies ran while one was open for 25% of the time, Pallas kernels for 0%

profile of v1, /device:TPU:0, one launch (start us, length us, event | category | flops | bytes accessed | tf_op | source)
XLA Modules:
  0.0 393.5 jit_solution(15858566617171104322)
XLA Ops:
  8.1 5.4 %reduce-window.6 = f32[3,1,6,2,128]{4,3,2,1,0:T(2,128)S(1)} reduce-window(f32[3,1,6,2,128]{4,3,2,1,0:T(2,128)S(1)} %bitcast.295, f32[]{:T(128)} %constant.193.clone.1), window={size=1x1x1x1x128 pad=0_0x0_0x0_0x0_0x127_0}, to_apply=%region_0.1 | reduce-window | flops 585216 | bytes 36868 | tf_op jit(solution)/shard_map/reduce-window
  14.0 1.1 fusion.94
  17.7 2.2 fusion.72
  20.9 3.0 collective-permute-start
  23.9 11.4 %collective-permute-done = bf16[1,256,768]{2,1,0:T(8,128)(2,1)} collective-permute-done((bf16[1,256,768]{2,1,0:T(8,128)(2,1)S(1)}, bf16[1,256,768]{2,1,0:T(8,128)(2,1)}, u32[]{:S(2)}, u32[]{:S(2)}) %collective-permute-start) | collective-permute-done | bytes 393248 | tf_op jit(solution)/shard_map/ppermute | solution.py:145
  35.3 2.1 collective-permute-start.1
  37.5 1.7 copy.120
  39.2 35.5 %all-gather.1 = f32[12,1,6,1]{2,3,1,0:T(1,128)} all-gather(f32[3,1,6,1]{2,3,1,0:T(1,128)S(1)} %copy.107), channel_id=3, replica_groups=mesh['groups'=2,'ctx'=4,'dp'=2,'mp'=2] {'ctx'}, dimensions={0}, use_global_device_ids=true | all-gather | bytes 360 | tf_op jit(solution)/shard_map/all_gather | solution.py:14
  74.9 15.2 %collective-permute-done.2 = bf16[1,256,768]{2,1,0:T(8,128)(2,1)S(1)} collective-permute-done((bf16[1,256,768]{2,1,0:T(8,128)(2,1)}, bf16[1,256,768]{2,1,0:T(8,128)(2,1)S(1)}, u32[]{:S(2)}, u32[]{:S(2)}) %collective-permute-start.2) | collective-permute-done | bytes 393248 | tf_op jit(solution)/shard_map/ppermute | solution.py:145
  90.2 1.0 constant_dynamic-update-slice_fusion.6
  91.2 1.0 constant_dynamic-update-slice_fusion.5
  92.3 1.0 constant_dynamic-update-slice_fusion.2
  93.3 1.0 constant_dynamic-update-slice_fusion.1
  94.5 2.9 gather_fusion
  97.4 2.9 gather_fusion.1
  100.3 5.8 %while.69 = (s32[]{:T(128)}, f32[3,1,6,64,128]{4,3,2,1,0:T(8,128)S(1)}, s32[]{:T(128)}, f32[4,3,1,6]{3,2,1,0:T(1,128)}, f32[4,3,1,6,64,128]{5,4,3,1,2,0:T(8,128)}, /*index=5*/s32[]{:T(128)}, s32[]{:T(128)}) while((s32[]{:T(128)}, f32[3,1,6,64,128]{4,3,2,1,0:T(8,128)S(1)}, s32[]{:T(128)}, f32[4,3,1,6]{3,2,1,0:T(1,128)}, ...), condition=%wide.region_5.6_spmd.clone, body=%wide.region_4.5_spmd.clone.sunk | while | flops 589828 | bytes 1769937 | solution.py:26
  101.0 1.2 fusion.187
  102.9 1.2 fusion.187
  104.8 1.2 fusion.187
  106.0 52.4 %all-gather.7.cloned.1.call-done = bf16[3,768,768]{2,1,0:T(8,128)(2,1)} async-done(((bf16[3,192,768]{2,1,0:T(8,128)(2,1)}), bf16[3,768,768]{2,1,0:T(8,128)(2,1)}) %all-gather.7.cloned.1.call-update) | async-done | bytes 3538960 | tf_op jit(solution)/shard_map/all_gather | solution.py:157
  158.4 3.4 fusion.71
  161.8 1.5 copy.104
  163.3 3.6 fusion.74
  167.2 27.0 %while.66 = (s32[]{:T(128)}, f32[3,1,6,64,128]{4,3,2,0,1:T(8,128)S(1)}, bf16[3,1,256,6,128]{2,4,3,0,1:T(8,128)(2,1)S(1)}, f32[2,3,1,6,64,128]{5,4,3,1,2,0:T(8,12...) while((s32[]{:T(128)}, ...), condition=%wide.region_8.9_spmd, body=%wide.region_6.8_spmd.sunk | while | flops 946094080 | bytes 10168943 | solution.py:99
  167.2 1.3 constant_dynamic-slice_fusion.11
  168.5 1.9 reduce_window_sum.68
  171.6 2.0 convolution_bitcast_fusion.8
  174.1 3.9 fusion.159
  178.2 2.5 fusion.157
  180.7 1.3 constant_dynamic-slice_fusion.11
  182.0 1.9 reduce_window_sum.68
  184.2 0.9 dynamic-slice_bitcast_fusion.6
  185.1 2.0 convolution_bitcast_fusion.8
  187.6 3.9 fusion.159
  191.6 2.5 fusion.157
  194.2 5.7 %fusion.82 = f32[3,768,768]{2,1,0:T(8,128)} fusion(bf16[3,256,768]{1,2,0:T(8,128)(2,1)S(1)} %bitcast.282, bf16[1,1,256,768]{3,2,0,1:T(8,128)(2,1)} %bitcast.292, bf16[1,1,256,768]{3,2,0,1:T(8,128)(2,1)} %bitcast.290, bf16[1,1,256,768]{3,2,0,1:T(8,128)(2,1)S(1)} %bitcast.287), kind=kOutput, calls=%fused_computation.120 | convolution fusion | flops 907149312 | bytes 9437184 | tf_op jit(solution)/shard_map/ovtd,ovti->odi/dot_general | solution.py:189
  201.2 1.8 copy.109
  203.0 13.1 %all-gather.9.cloned.1.call-done = f32[12,6,64,128]{3,2,1,0:T(8,128)} async-done(((f32[3,6,64,128]{3,2,1,0:T(8,128)}), f32[12,6,64,128]{3,2,1,0:T(8,128)}) %all-gather.9.cloned.1.call-update) | async-done | bytes 2359312 | tf_op jit(solution)/shard_map/all_gather | solution.py:14
  216.1 1.8 rev.6
  220.0 41.1 %while.67 = (s32[]{:T(128)}, f32[3,1,6,64,128]{4,3,2,0,1:T(8,128)S(1)}, bf16[3,1,256,6,128]{2,4,3,0,1:T(8,128)(2,1)S(1)}, f32[3,1,256,64]{2,3,0,1:T(8,128)}, f32...) while((s32[]{:T(128)}, ...), condition=%wide.region_12.13_spmd, body=%wide.region_9.12_spmd.sunk | while | flops 1929625600 | bytes 41488220 | solution.py:120
  221.1 1.1 dynamic-slice_bitcast_fusion.7
  222.2 2.0 convolution_bitcast_fusion.9
  224.9 1.7 fusion.178
  226.6 1.0 copy-done.4
  228.0 2.3 fusion.182
  230.3 3.7 fusion.180
  234.5 2.6 fusion.179
  237.2 2.4 fusion.176
  239.6 0.9 fusion.181
  241.6 1.1 dynamic-slice_bitcast_fusion.7
  242.7 2.0 convolution_bitcast_fusion.9
  245.4 1.7 fusion.178
  247.1 1.0 copy-done.4
  248.5 2.3 fusion.182
  250.8 3.7 fusion.180
  255.0 2.7 fusion.179
  257.7 2.4 fusion.176
  260.2 0.9 fusion.181
  261.1 1.1 copy.121
  262.2 1.1 copy.122
  263.5 1.5 copy.125
  265.0 5.0 %all-reduce.3 = bf16[3,1,256,128]{3,2,1,0:T(8,128)(2,1)} all-reduce(f32[3,1,256,128]{3,2,1,0:T(8,128)S(1)} %pad_maximum_fusion), channel_id=1, replica_groups=mesh['groups'=2,'ctx'=4,'dp'=2,'mp'=2] {'mp'}, use_global_device_ids=true, to_apply=%region_13.14 | all-reduce | flops 98304 | bytes 589824 | tf_op jit(solution)/shard_map/psum | solution.py:184
  270.0 70.6 %reduce-scatter.2.cloned.1.call-done = f32[3,192,768]{2,1,0:T(8,128)} async-done(((f32[3,768,768]{2,1,0:T(8,128)}), f32[3,192,768]{2,1,0:T(8,128)}) %reduce-scatter.2.cloned.1.call-update) | async-done | bytes 1769488 | tf_op jit(solution)/shard_map/reduce_scatter | solution.py:192
  340.6 46.3 %all-reduce.2 = bf16[3,192,768]{2,1,0:T(8,128)(2,1)} all-reduce(f32[3,192,768]{2,1,0:T(8,128)} %reduce-scatter.2.cloned.1.call-done), channel_id=1, replica_groups=mesh['groups'=2,'ctx'=4,'dp'=2,'mp'=2] {'dp'}, use_global_device_ids=true, to_apply=%region_15.16 | all-reduce | flops 442368 | bytes 2654208 | tf_op jit(solution)/shard_map/psum | solution.py:193
  (133 shorter events, 19.4 us)
Async XLA Ops:
  7.2 8.2 %copy-start.10 = (bf16[3,1,256,768]{3,2,1,0:T(8,128)(2,1)S(1)}, bf16[3,1,256,768]{3,2,1,0:T(8,128)(2,1)}, u32[]{:S(2)}) copy-start(bf16[3,1,256,768]{3,2,1,0:T(8,128)(2,1)} %param.14) | copy-start | bytes 3538948
  7.2 93.1 %all-gather.11.cloned.1.call-start = ((), (), s32[]{:S(2)}) async-start(), calls=%async_computation.4 | async-start | bytes 2949120 | tf_op jit(solution)/shard_map/all_gather | solution.py:14
  8.0 8.0 %copy-start.8 = (f32[3,1,6,256]{3,2,1,0:T(8,128)}, f32[3,1,6,256]{3,2,1,0:T(8,128)S(1)}, u32[]{:S(2)}) copy-start(f32[3,1,6,256]{3,2,1,0:T(8,128)S(1)} %fusion.84) | copy-start | bytes 55300
  19.9 1.0 copy-start.6
  19.9 138.5 %all-gather.7.cloned.1.call-start = ((), (), s32[]{:S(2)}) async-start(), calls=%async_computation.1 | async-start | bytes 4423680 | tf_op jit(solution)/shard_map/all_gather | solution.py:157
  20.6 195.5 %all-gather.9.cloned.1.call-start = ((), (), s32[]{:S(2)}) async-start(), calls=%async_computation.3 | async-start | bytes 2949120 | tf_op jit(solution)/shard_map/all_gather | solution.py:14
  20.9 14.4 %collective-permute-start = (bf16[1,256,768]{2,1,0:T(8,128)(2,1)S(1)}, bf16[1,256,768]{2,1,0:T(8,128)(2,1)}, u32[]{:S(2)}, u32[]{:S(2)}) collective-permute-start(bf16[1,256,768]{2,1,0:T(8,128)(2,1)S(1)} %copy-done.6), channel_id=1, source_target_pairs={{0,4},{4,8},{8,12},{12,0},{1,5},{5,9},{9,13},{13,1},{2,6},{6,10},{... | collective-permute-start | bytes 1179656 | tf_op jit(solution)/shard_map/ppermute | solution.py:145
  35.3 39.5 %collective-permute-start.1 = (bf16[1,256,768]{2,1,0:T(8,128)(2,1)}, bf16[1,256,768]{2,1,0:T(8,128)(2,1)}, u32[]{:S(2)}, u32[]{:S(2)}) collective-permute-start(bf16[1,256,768]{2,1,0:T(8,128)(2,1)} %collective-permute-done), channel_id=1, source_target_pairs={{0,4},{4,8},{8,12},{12,0},{1,5},{5,9},{9,13},{13,1},{2,6},{6,10},{... | collective-permute-start | bytes 1179656 | tf_op jit(solution)/shard_map/ppermute | solution.py:145
  37.5 37.3 %copy-start.14 = (s32[2,1,256]{2,1,0:T(1,128)S(1)}, s32[2,1,256]{2,1,0:T(1,128)}, u32[]{:S(2)}) copy-start(s32[2,1,256]{2,1,0:T(1,128)} %param.17) | copy-start | bytes 6148
  74.8 15.3 %collective-permute-start.2 = (bf16[1,256,768]{2,1,0:T(8,128)(2,1)}, bf16[1,256,768]{2,1,0:T(8,128)(2,1)S(1)}, u32[]{:S(2)}, u32[]{:S(2)}) collective-permute-start(bf16[1,256,768]{2,1,0:T(8,128)(2,1)} %collective-permute-done.1), channel_id=1, source_target_pairs={{0,4},{4,8},{8,12},{12,0},{1,5},{5,9},{9,13},{13,1},{2,6},{6,10},{... | collective-permute-start | bytes 1179656 | tf_op jit(solution)/shard_map/ppermute | solution.py:145
  100.3 58.1 %copy-start.7 = (bf16[1,256,768]{2,1,0:T(8,128)(2,1)S(1)}, bf16[1,256,768]{2,1,0:T(8,128)(2,1)}, u32[]{:S(2)}) copy-start(bf16[1,256,768]{2,1,0:T(8,128)(2,1)} %param.18) | copy-start | bytes 1179652
  161.8 1.5 copy-start.2
  166.8 173.8 %reduce-scatter.2.cloned.1.call-start = ((), (), s32[]{:S(2)}) async-start(), calls=%async_computation.2 | async-start | bytes 8847360 | tf_op jit(solution)/shard_map/reduce_scatter | solution.py:192
  194.2 5.7 %copy-start.1 = (f32[2,3,1,6,64,128]{5,4,3,1,2,0:T(8,128)}, f32[2,3,1,6,64,128]{5,4,3,1,2,0:T(8,128)S(1)}, u32[]{:S(2)}) copy-start(f32[2,3,1,6,64,128]{5,4,3,1,2,0:T(8,128)S(1)} %get-tuple-element.1132) | copy-start | bytes 3538948
  199.9 0.7 copy-start.13
  199.9 1.3 copy-start.3
  218.5 1.5 copy-start.9
  221.1 3.6 copy-start
  226.6 1.0 copy-start.4
  230.3 3.7 copy-start.11
  234.5 2.6 copy-start.12
  237.2 3.4 copy-start.5
  241.6 3.6 copy-start
  247.1 1.0 copy-start.4
  250.8 3.7 copy-start.11
  255.0 2.7 copy-start.12
  257.7 3.4 copy-start.5
Sparse Core Ops, SparseCore 0:
  20.0 68.4 all-gather.10
  90.1 68.3 all-gather.6
  167.0 49.1 all-gather.8
  218.3 122.3 reduce-scatter.1
